TPU v7x, 32 devices: a whole 2x2x4 slice. The times are simulated.
32 devices in a mesh: row: 8 (over z, core), col: 4 (over y, x).
Axes of the slice: x: 2, y: 2, z: 4, core: 2. Of those that a mesh axis runs over, the one named last changes fastest.
Arguments:
- trailing: float32 [4, 8, 512, 8, 4, 512], P(None, 'row', None, None, 'col'), as said below
Outputs:
- factor: float32 [4, 8, 512, 8, 4, 512], P(None, 'row', None, None, 'col')
Inputs may be any that keep to these rules, and one draw needn't show every extreme that they name: trailing is symmetric and positive definite, with entries of at least 0.
All inputs are finite; a program needn't handle non-finite values.
Results may differ from a plain program's by a relative error of at most 0.0003.
Values sent between devices are 32-bit elements; how exact they have to be, the bound alone decides.
A program may use at most 192 MiB of HBM per device.

v0:
```python
import jax
import jax.numpy as jnp
from jax import lax
from jax.sharding import PartitionSpec as P

IB = 128
STEPS = 2


def spread(shard, axis, root):
    mine = lax.axis_index(axis) == root
    return lax.psum(jnp.where(mine, shard, jnp.zeros_like(shard)), axis)


def tri_inverse(lower_tri, block_size):
    block_count = lower_tri.shape[0] // block_size
    identity = jnp.eye(block_size, dtype=lower_tri.dtype)

    def piece_of(p, q):
        return lower_tri[
            p * block_size : (p + 1) * block_size, q * block_size : (q + 1) * block_size
        ]

    inverse = [
        [jnp.zeros((block_size, block_size), lower_tri.dtype) for q in range(block_count)]
        for p in range(block_count)
    ]
    for p in range(block_count):
        inverse[p][p] = lax.linalg.triangular_solve(
            piece_of(p, p), identity, left_side=True, lower=True
        )
    for p in range(block_count):
        for q in range(p):
            partial_sum = jnp.zeros((block_size, block_size), lower_tri.dtype)
            for s in range(q, p):
                partial_sum = partial_sum + jnp.dot(
                    piece_of(p, s), inverse[s][q], precision=lax.Precision.HIGHEST
                )
            inverse[p][q] = -jnp.dot(inverse[p][p], partial_sum, precision=lax.Precision.HIGHEST)
    return jnp.block(inverse)


def solve_panel(column, inverse):
    return jnp.einsum("iab,cb->iac", column, inverse, precision=lax.Precision.HIGHEST)


def full_update(local_tiles, panel_tiles, across, allowed):
    product = jnp.einsum("iab,jcb->iajc", panel_tiles, across, precision=lax.Precision.HIGHEST)
    return local_tiles - jnp.where(allowed[:, None, :, None], product, 0.0)


def local(trailing):
    row_tiles = trailing.shape[0]
    tile_size = trailing.shape[2]
    col_tiles = trailing.shape[3]
    n_row = lax.axis_size("row")
    n_col = lax.axis_size("col")
    row_index = lax.axis_index("row")
    col_index = lax.axis_index("col")
    local_tiles = trailing.reshape(row_tiles, tile_size, col_tiles, tile_size)
    global_rows = jnp.arange(row_tiles, dtype=jnp.int32) * n_row + row_index
    global_cols = jnp.arange(col_tiles, dtype=jnp.int32) * n_col + col_index
    column = local_tiles[:, :, 0, :]
    for k in range(STEPS):
        local_row = k // n_row
        local_col = k // n_col
        diagonal = spread(column[local_row], "row", k % n_row)
        factor_kk = jnp.linalg.cholesky(diagonal)
        solved = solve_panel(column, tri_inverse(factor_kk, IB))
        panel_tiles = spread(solved, "col", k % n_col)
        live_rows = (global_rows > k)[:, None, None]
        panel_tiles = jnp.where(live_rows, panel_tiles, 0.0)
        received = []
        for j in range(col_tiles):
            target = j * n_col + col_index
            piece_tile = lax.dynamic_index_in_dim(panel_tiles, target // n_row, 0, keepdims=False)
            received.append(spread(piece_tile, "row", target % n_row))
        across = jnp.stack(received)
        new_column = jnp.where(
            live_rows,
            panel_tiles,
            jnp.where((global_rows == k)[:, None, None], jnp.tril(factor_kk)[None], column),
        )
        local_tiles = local_tiles.at[:, :, local_col, :].set(
            jnp.where(global_cols[local_col] == k, new_column, local_tiles[:, :, local_col, :])
        )
        allowed = (global_rows[:, None] >= global_cols[None, :]) & (global_cols[None, :] > k)
        next_col = (k + 1) // n_col
        local_tiles = full_update(local_tiles, panel_tiles, across, allowed)
        if k + 1 < STEPS:
            column = local_tiles[:, :, next_col, :]
    keep_tiles = global_rows[:, None, None, None] >= global_cols[None, None, :, None]
    result = jnp.where(keep_tiles, local_tiles, 0.0)
    return result.reshape(row_tiles, 1, tile_size, col_tiles, 1, tile_size)


def solution(mesh):
    in_specs = (P(None, "row", None, None, "col", None),)
    out_specs = P(None, "row", None, None, "col", None)
    return jax.shard_map(local, mesh=mesh, in_specs=in_specs, out_specs=out_specs, check_vma=False)
```

profile of v0, /device:TPU:28, one launch (start us, length us, event | category | flops | bytes accessed | tf_op | source)
XLA Modules:
  0.0 1323.5 jit_solution(1569448012670204149)
XLA Ops:
  6.5 78.2 %copy.2 = f32[4,1,512,8,1,512]{2,5,3,0,4,1:T(8,128)} copy(f32[4,1,512,8,1,512]{5,4,3,2,1,0:T(1,128)} %param.24) | data formatting | bytes 67108864 | tf_op args[0]
  84.8 2.3 fusion.16
  87.1 78.7 %copy.34 = f32[4,1,512,8,1,512]{2,5,0,3,1,4:T(8,128)} copy(f32[4,1,512,8,1,512]{5,4,3,2,1,0:T(1,128)} %param.24) | data formatting | bytes 67108864 | tf_op jit(solution)/shard_map/reshape | solution.py:60
  165.8 1.6 copy.3
  167.4 1.4 fusion.50
  168.9 11.7 cholesky.286
  180.6 9.8 custom-call.33
  191.2 11.7 cholesky.305
  203.0 10.2 custom-call.34
  213.9 11.7 cholesky.326
  226.3 9.8 custom-call.35
  236.8 11.7 cholesky.343
  252.9 9.8 custom-call.36
  263.8 9.8 custom-call.37
  274.8 9.8 custom-call.38
  285.9 9.8 custom-call.39
  297.8 10.5 select_bitcast_fusion.1
  308.9 104.2 %all-reduce.12.cloned.1.call-done = f32[4,512,512]{1,2,0:T(8,128)} async-done(((f32[4,512,512]{1,2,0:T(8,128)}), f32[4,512,512]{1,2,0:T(8,128)}) %all-reduce.12.cloned.1.call-update) | async-done | bytes 4194320 | tf_op jit(solution)/shard_map/psum | solution.py:12
  413.1 6.7 bitcast_dynamic-update-slice_fusion
  419.8 3.7 dynamic-slice_select_fusion.8
  424.6 177.5 %all-reduce.20.cloned.1.call-done = (f32[1,512,512]{1,2,0:T(8,128)}, f32[1,512,512]{1,2,0:T(8,128)}, f32[1,512,512]{1,2,0:T(8,128)}, f32[1,512,512]{1,2,0:T(8,12...) async-done(((f32[1,512,512]{1,2,0:T(8,128)}, f32[1,512,512]{1,2,0:T(8,128)}, f32[1,512,512]{1,2,0:T(8,128)}, ...) | async-done | bytes 8388624 | tf_op jit(solution)/shard_map/psum | solution.py:12
  602.1 1.4 constant_dynamic-update-slice_fusion.7
  603.6 2.0 constant_dynamic-update-slice_fusion.6
  608.5 62.8 %select_subtract_fusion = f32[4,512,8,512]{1,3,2,0:T(8,128)} fusion(f32[4,512,8,512]{1,3,2,0:T(8,128)} %get-tuple-element.54, pred[4,8]{1,0:T(4,128)(4,1)S(1)} %broadcast_and_fusion.1, f32[8,512,512]{1,2,0:T(8,128)S(1)} %constant_dynamic-update-slice_fusion, f32[4,512,512]{1,2,0:T(8,128)S(1)} %copy-done.3), kind=kOutput, calls=%fused_computation.1 | convolution fusion | flops 51556384768 | bytes 79691808 | tf_op jit(solution)/shard_map/iab,jcb->iajc/dot_general | solution.py:48
  671.3 2.3 fusion.15
  673.9 57.6 %all-reduce.14.cloned.1.call-done = f32[512,512]{0,1:T(8,128)} async-done(((f32[512,512]{0,1:T(8,128)}), f32[512,512]{0,1:T(8,128)}) %all-reduce.14.cloned.1.call-update) | async-done | bytes 1048592 | tf_op jit(solution)/shard_map/psum | solution.py:12
  731.5 1.6 copy.13
  733.0 1.4 fusion.49
  734.5 11.7 cholesky.358
  746.4 9.8 custom-call.40
  756.9 11.7 cholesky.377
  770.0 10.0 custom-call.41
  780.6 11.7 cholesky.398
  793.0 9.8 custom-call.42
  803.4 11.7 cholesky.415
  819.1 9.8 custom-call.43
  830.0 9.8 custom-call.44
  840.9 9.8 custom-call.45
  852.1 9.8 custom-call.46
  863.9 10.3 convolution_select_fusion
  874.4 4.6 slice_bitcast_fusion
  879.3 99.8 %all-reduce.16.cloned.1.call-done = f32[4,512,512]{1,2,0:T(8,128)} async-done(((f32[4,512,512]{1,2,0:T(8,128)}), f32[4,512,512]{1,2,0:T(8,128)}) %all-reduce.16.cloned.1.call-update) | async-done | bytes 4194320 | tf_op jit(solution)/shard_map/psum | solution.py:12
  979.1 6.7 bitcast_dynamic-update-slice_fusion.1
  985.8 3.7 dynamic-slice_select_fusion
  990.5 177.6 %all-reduce.18.cloned.1.call-done = (f32[1,512,512]{1,2,0:T(8,128)}, f32[1,512,512]{1,2,0:T(8,128)}, f32[1,512,512]{1,2,0:T(8,128)}, f32[1,512,512]{1,2,0:T(8,12...) async-done(((f32[1,512,512]{1,2,0:T(8,128)}, f32[1,512,512]{1,2,0:T(8,128)}, f32[1,512,512]{1,2,0:T(8,128)}, ...) | async-done | bytes 8388624 | tf_op jit(solution)/shard_map/psum | solution.py:12
  1169.6 2.0 constant_dynamic-update-slice_fusion.14
  1174.5 63.7 %select_bitcast_fusion = f32[4,1,512,8,1,512]{2,5,3,0,4,1:T(8,128)} fusion(f32[4,512,8,512]{1,3,2,0:T(8,128)} %get-tuple-element.50, pred[4,8]{1,0:T(4,128)(4,1)S(1)} %get-tuple-element.48, pred[4,8]{1,0:T(4,128)(4,1)S(1)} %get-tuple-element.49, f32[8,512,512]{1,2,0:T(8,128)S(1)} %constant_dynamic-update-slice_fusion.8, f32[4,512,512]{1,2,0:T(8,128)S(1)} %copy-done.1), kind=kOutput, calls=%fused_computation | convolution fusion | flops 51564773376 | bytes 79691840 | tf_op jit(solution)/shard_map/iab,jcb->iajc/dot_general | solution.py:48
  1238.2 78.2 %copy.21 = f32[4,1,512,8,1,512]{5,4,3,2,1,0:T(1,128)} copy(f32[4,1,512,8,1,512]{2,5,3,0,4,1:T(8,128)} %select_bitcast_fusion) | data formatting | bytes 67108864 | tf_op jit(solution)/shard_map/reshape | solution.py:94
  (140 shorter events, 31.5 us)
Async XLA Ops:
  6.5 159.3 %all-reduce.10.cloned.1.call-start = ((), (), s32[]{:S(2)}) async-start(), calls=%async_computation | async-start | bytes 2097152 | tf_op jit(solution)/shard_map/psum | solution.py:12
  87.1 326.0 %all-reduce.12.cloned.1.call-start = ((), (), s32[]{:S(2)}) async-start(), calls=%async_computation.1 | async-start | bytes 8388608 | tf_op jit(solution)/shard_map/psum | solution.py:12
  308.3 293.8 %all-reduce.20.cloned.1.call-start = ((), (), s32[]{:S(2)}) async-start(), calls=%async_computation.5 | async-start | bytes 16777216 | tf_op jit(solution)/shard_map/psum | solution.py:12
  419.8 4.6 copy-start.2
  424.5 307.0 %all-reduce.14.cloned.1.call-start = ((), (), s32[]{:S(2)}) async-start(), calls=%async_computation.2 | async-start | bytes 2097152 | tf_op jit(solution)/shard_map/psum | solution.py:12
  602.1 6.0 copy-start.7
  602.1 6.1 copy-start.6
  602.1 6.2 copy-start.5
  602.1 6.3 copy-start.4
  602.1 6.4 copy-start.3
  673.6 305.5 %all-reduce.16.cloned.1.call-start = ((), (), s32[]{:S(2)}) async-start(), calls=%async_computation.3 | async-start | bytes 8388608 | tf_op jit(solution)/shard_map/psum | solution.py:12
  874.3 293.8 %all-reduce.18.cloned.1.call-start = ((), (), s32[]{:S(2)}) async-start(), calls=%async_computation.4 | async-start | bytes 16777216 | tf_op jit(solution)/shard_map/psum | solution.py:12
  985.8 4.6 copy-start
  1168.1 6.0 copy-start.11
  1168.1 6.1 copy-start.10
  1168.1 6.2 copy-start.9
  1168.1 6.3 copy-start.8
  1168.1 6.4 copy-start.1
Sparse Core Ops, SparseCore 0:
  87.2 57.7 all-reduce.9
  308.4 104.6 all-reduce.11
  424.6 177.4 all-reduce.19
  673.8 57.6 all-reduce.13
  874.4 104.6 all-reduce.15
  990.6 177.4 all-reduce.17
where the time goes:
time: 1340 us; the launch traced here: 1320 us
  waiting for transfers between devices  617 us (46%)
  other arithmetic  266 us (20%)
  local copies, waits for them, and re-layouts  258 us (19%)
  matrix products  162 us (12%)
  between operations  19.8 us (1%)
    psum x6, waiting for transfers between devices, spread(): return lax.psum(jnp.where(mine, shard, jnp.zeros_like(shard)), axis)  617 us
    another operation x29, other arithmetic, local(): factor_kk = jnp.linalg.cholesky(diagonal)  158 us
    dot_general x2, matrix products, full_update(): jnp.einsum('iab,jcb->iajc', panel_tiles, across, precision=lax.Precision....  126 us
    unnamed x39, local copies, waits for them, and re-layouts  92.5 us
    reshape x1, local copies, waits for them, and re-layouts, local(): local_tiles = trailing.reshape(row_tiles, tile_size, col_tiles, tile_size)  78.7 us
    another operation x10, other arithmetic, tri_inverse(): lax.linalg.triangular_solve(piece_of(p, p), identity, left_side=True, low...  78.5 us
    reshape x1, local copies, waits for them, and re-layouts, local(): return result.reshape(row_tiles, 1, tile_size, col_tiles, 1, tile_size)  78.2 us
  transfers between devices with their start and end apart: 6, of which 5 were waited for; matrix products, arithmetic and copies ran while one was open for 6% of the time, Pallas kernels for 0%

commit v1 on v0

v1 whole, which is shorter than its diff:
```python
import functools

import jax
import jax.numpy as jnp
from jax import lax
from jax.experimental import pallas as pl
from jax.experimental.pallas import tpu as pltpu
from jax.sharding import PartitionSpec as P

IB = 128
STEPS = 2
HIGHEST = lax.Precision.HIGHEST


def eliminate(block):
    n = IB
    groups = n // 8
    rows = [block[8 * g : 8 * g + 8, :] for g in range(groups)]
    lane = lax.broadcasted_iota(jnp.int32, (1, n), 1)
    sub = lax.broadcasted_iota(jnp.int32, (8, 1), 0)
    for j in range(n):
        g0, jj = j // 8, j % 8
        row = rows[g0][jj : jj + 1, :]
        inv = 1.0 / row[:, j : j + 1]
        here = lane == j
        pivot_row = jnp.where(here, 1.0, row)
        for g in range(g0, groups):
            if g == g0 and jj == 7:
                continue
            factor = rows[g][:, j : j + 1] * inv
            if g == g0:
                below = sub > jj
                factor = jnp.where(below, factor, 0.0)
                base = jnp.where(here & below, 0.0, rows[g])
            else:
                base = jnp.where(here, 0.0, rows[g])
            rows[g] = base - factor * pivot_row
    full = jnp.concatenate(rows, axis=0)
    r = lax.broadcasted_iota(jnp.int32, (n, n), 0)
    c = lax.broadcasted_iota(jnp.int32, (n, n), 1)
    diag = jnp.sum(jnp.where(r == c, full, 0.0), axis=1, keepdims=True)
    root = 1.0 / jnp.sqrt(diag)
    scaled = full * root
    return jnp.where(c < r, scaled, jnp.where(c == r, root, 0.0))


def factor_kernel(stages, at_ref, a_ref, t_ref):
    n = a_ref.shape[0]
    count = n // IB
    t_ref[...] = a_ref[...]
    block_of = lax.broadcasted_iota(jnp.int32, (IB, n), 1) // IB
    begin = at_ref[0]

    def stage(step, carry):
        p = begin + step
        at = pl.ds(pl.multiple_of(p * IB, IB), IB)
        w = eliminate(t_ref[at, at])
        pre = t_ref[at, :]
        done = jnp.dot(w, pre, precision=HIGHEST, preferred_element_type=jnp.float32)
        t_ref[at, :] = done
        t_ref[at, at] = w
        fresh = t_ref[at, :]

        def row(i, inner):
            to = pl.ds(pl.multiple_of(i * IB, IB), IB)
            lower = t_ref[at, to]
            delta = lax.dot_general(
                lower, fresh, (((0,), (0,)), ((), ())),
                precision=HIGHEST, preferred_element_type=jnp.float32,
            )
            t_ref[to, :] = jnp.where(block_of == p, 0.0, t_ref[to, :]) - delta
            return inner

        lax.fori_loop(p + 1, count, row, 0)
        return carry

    lax.fori_loop(0, stages, stage, 0)


def factor_part(square, begin, stages):
    n = square.shape[0]
    return pl.pallas_call(
        functools.partial(factor_kernel, stages),
        out_shape=jax.ShapeDtypeStruct((n, n), jnp.float32),
        in_specs=[
            pl.BlockSpec(memory_space=pltpu.SMEM),
            pl.BlockSpec(memory_space=pltpu.VMEM),
        ],
        out_specs=pl.BlockSpec(memory_space=pltpu.VMEM),
        compiler_params=pltpu.CompilerParams(vmem_limit_bytes=24 * 1024 * 1024),
        cost_estimate=pl.CostEstimate(
            flops=15_000_000_000 * stages // 2, bytes_accessed=2 * n * n * 4, transcendentals=0
        ),
        name="factor",
    )(jnp.full((1,), begin, jnp.int32), square)


def split(x):
    hi = x.astype(jnp.bfloat16)
    lo = (x - hi.astype(jnp.float32)).astype(jnp.bfloat16)
    return hi, lo


def rows_kernel(x_ref, y_ref, w_ref, p_ref, h_ref, l_ref):
    b = x_ref.shape[1]
    dot = functools.partial(
        lax.dot_general, dimension_numbers=(((1,), (1,)), ((), ())),
        precision=HIGHEST, preferred_element_type=jnp.float32,
    )
    x, y = x_ref[0], y_ref[0]
    first = dot(x, w_ref[:b, :b])
    second = dot(x, w_ref[b:, :b]) + dot(y, w_ref[b:, b:])
    for at, value in ((0, first), (b, second)):
        hi, lo = split(value)
        p_ref[0, :, at : at + b] = value
        h_ref[0, :, at : at + b] = hi
        l_ref[0, :, at : at + b] = lo


def cols_kernel(x_ref, y_ref, w_ref, h_ref, l_ref):
    b = x_ref.shape[1]
    dot = functools.partial(
        jnp.dot, precision=HIGHEST, preferred_element_type=jnp.float32
    )
    x, y = x_ref[0], y_ref[0]
    first = dot(w_ref[:b, :b], x)
    second = dot(w_ref[b:, :b], x) + dot(w_ref[b:, b:], y)
    for at, value in ((0, first), (b, second)):
        hi, lo = split(value)
        h_ref[0, at : at + b, :] = hi
        l_ref[0, at : at + b, :] = lo


def solve(kernel, x, y, w, shapes, name):
    m, b, _ = x.shape
    tile = pl.BlockSpec((1, b, b), lambda i: (i, 0, 0))
    return pl.pallas_call(
        kernel,
        out_shape=[jax.ShapeDtypeStruct((m, *shape), dtype) for shape, dtype in shapes],
        grid=(m,),
        in_specs=[tile, tile, pl.BlockSpec(memory_space=pltpu.VMEM)],
        out_specs=[pl.BlockSpec((1, *shape), lambda i: (i, 0, 0)) for shape, _ in shapes],
        compiler_params=pltpu.CompilerParams(vmem_limit_bytes=44 * 1024 * 1024),
        cost_estimate=pl.CostEstimate(
            flops=m * 36 * b**3, bytes_accessed=m * b * b * 24, transcendentals=0
        ),
        name=name,
    )(x, y, w)


def update_kernel(n_row, n_col, at_ref, a_ref, ph_ref, pl_ref, qh_ref, ql_ref, new_ref, o_ref):
    i, j = pl.program_id(0), pl.program_id(1)
    t = i * n_row + at_ref[0]
    s = j * n_col + at_ref[1]

    @pl.when(t < s)
    def _():
        o_ref[...] = jnp.zeros_like(o_ref)

    @pl.when((t >= s) & (s < STEPS))
    def _():
        o_ref[...] = new_ref[...].reshape(o_ref.shape)

    @pl.when((t >= s) & (s >= STEPS))
    def _():
        dot = functools.partial(jnp.dot, preferred_element_type=jnp.float32)
        qh, ql = qh_ref[j], ql_ref[j]
        ph, plo = ph_ref[0], pl_ref[0]
        acc = dot(ph, qh) + (dot(ph, ql) + dot(plo, qh))
        o_ref[...] = a_ref[...] - acc.reshape(o_ref.shape)


def update(trailing, place, panel, across, new_column, n_row, n_col):
    rows, _, b, cols, _, _ = trailing.shape
    ph, plo = panel
    qh, ql = across
    depth = ph.shape[-1]

    def needed(i, j, at):
        last = jnp.maximum((i * n_row + at[0] - at[1]) // n_col, 0)
        return jnp.minimum(j, jnp.minimum(last, cols - 1))

    tile = (1, 1, b, 1, 1, b)
    whole = pl.BlockSpec(memory_space=pltpu.VMEM)
    return pl.pallas_call(
        functools.partial(update_kernel, n_row, n_col),
        out_shape=jax.ShapeDtypeStruct(trailing.shape, jnp.float32),
        grid_spec=pltpu.PrefetchScalarGridSpec(
            num_scalar_prefetch=1,
            grid=(rows, cols),
            in_specs=[
                pl.BlockSpec(tile, lambda i, j, at: (i, 0, 0, needed(i, j, at), 0, 0)),
                pl.BlockSpec((1, b, depth), lambda i, j, at: (i, 0, 0)),
                pl.BlockSpec((1, b, depth), lambda i, j, at: (i, 0, 0)),
                whole,
                whole,
                pl.BlockSpec((1, b, b), lambda i, j, at: (i, 0, 0)),
            ],
            out_specs=pl.BlockSpec(tile, lambda i, j, at: (i, 0, 0, j, 0, 0)),
        ),
        compiler_params=pltpu.CompilerParams(vmem_limit_bytes=48 * 1024 * 1024),
        name="update",
    )(place, trailing, ph, plo, qh, ql, new_column)


def corner_square(seed):
    a00, a10, a11 = seed
    return jnp.block([[a00, a10.T], [a10, a11]])


def local(trailing):
    row_tiles, _, b, col_tiles, _, _ = trailing.shape
    n_row = lax.axis_size("row")
    n_col = lax.axis_size("col")
    r = lax.axis_index("row")
    c = lax.axis_index("col")
    own = trailing[:, 0, :, 0, 0, :]
    corner = own[0]
    seed = [
        jnp.where((r == t) & (c == s), corner, 0.0) for t, s in ((0, 0), (1, 0), (1, 1))
    ]
    seed = lax.psum(jnp.stack(seed), ("row", "col"))

    z = r // 2
    hops = n_row // 2 - 1
    steps = col_tiles + hops - 1
    tiles = [trailing[0, 0, :, j, 0, :] for j in range(col_tiles)]
    arrived = tiles[0]
    parts = 4
    per = 2 * b // IB // parts
    gate = min(3, steps)
    square = None
    work = 0
    held = own
    keep = {}
    for step in range(steps):
        if step == gate:
            arrived, seed, own_late = lax.optimization_barrier((arrived, seed, own))
            square = corner_square(seed)
            held = own_late
        elif step > gate and work < parts:
            arrived, square = lax.optimization_barrier((arrived, square))
        head = tiles[step] if step < col_tiles else tiles[-1]
        send = jnp.where(z == 0, head, arrived)
        arrived = lax.ppermute(send, "row", [(x, x + 2) for x in range(n_row - 2)])
        keep[step] = arrived
        if step >= gate and work < parts:
            square = factor_part(square, work * per, per)
            work += 1
    if square is None:
        square = corner_square(seed)
    while work < parts:
        square = factor_part(square, work * per, per)
        work += 1
    columns = []
    for j in range(col_tiles):
        tile = tiles[j]
        for hop in range(1, hops + 1):
            tile = jnp.where(z == hop, keep[j + hop - 1], tile)
        columns.append(tile)
    columns = jnp.stack(columns)
    swapped = lax.ppermute(columns, "row", [(x, x ^ 1) for x in range(n_row)])
    first_row = r % 2 == 0
    top = jnp.where(first_row, columns, swapped)
    bottom = jnp.where(first_row, swapped, columns)

    d = 2
    while d < n_col:
        more = lax.ppermute(held, "col", [(x, x + d) for x in range(d)])
        held = jnp.where((c >= d) & (c < 2 * d), more, held)
        d *= 2
    other = lax.ppermute(held, "col", [(x, x ^ 1) for x in range(n_col)])
    even = c % 2 == 0
    left = jnp.where(even, held, other)
    right = jnp.where(even, other, held)

    block = jnp.arange(2 * b) // IB
    w = jnp.where(block[:, None] >= block[None, :], square, 0.0)
    f32, bf16 = jnp.float32, jnp.bfloat16
    wide, tall = (b, 2 * b), (2 * b, b)
    panel, *halves = solve(
        rows_kernel, left, right, w, [(wide, f32), (wide, bf16), (wide, bf16)], "rows"
    )
    across = solve(cols_kernel, top, bottom, w, [(tall, bf16), (tall, bf16)], "cols")
    mine_col = jnp.where(c == 0, panel[:, :, :b], panel[:, :, b:])
    rows_at = jnp.arange(row_tiles, dtype=jnp.int32) * n_row + r
    new_column = jnp.where((rows_at == c)[:, None, None], jnp.tril(mine_col), mine_col)
    place = jnp.stack([r, c]).astype(jnp.int32)
    return update(trailing, place, halves, across, new_column, n_row, n_col)


def solution(mesh):
    spec = P(None, "row", None, None, "col", None)
    return jax.shard_map(local, mesh=mesh, in_specs=(spec,), out_specs=spec, check_vma=False)
```

time: 1340 us -> 702 us (0.52)
  waiting for transfers between devices: 617 us -> 317 us
  Pallas kernels: 0 us -> 240 us
  local copies, waits for them, and re-layouts: 258 us -> 33.5 us
  other arithmetic: 266 us -> 70.8 us
  matrix products: 162 us -> 0 us
  starting transfers between devices: 0.38 us -> 17.9 us
    psum x6 -> x1, waiting for transfers between devices: 617 us -> 101 us  [local(): seed = lax.psum(jnp.stack(seed), ('row', 'col'))]
    pallas_call x0 -> x7, Pallas kernels: none -> 240 us  [the longest x4 109 us: factor_part(): pl.pallas_call(functools.partial(factor_kernel, stages), out_shape=jax.Sh...]
    another operation x39 -> x3, other arithmetic: 237 us -> 5.4 us  [the longest x1 3.86 us: local(): seed = lax.psum(jnp.stack(seed), ('row', 'col'))]
    ppermute x0 -> x13, waiting for transfers between devices: none -> 216 us  [the longest x10 136 us: local(): arrived = lax.ppermute(send, 'row', [(x, x + 2) for x in range(n_row - 2)])]
    reshape x2 -> x0, local copies, waits for them, and re-layouts: 157 us -> none  [the longest x1 78.7 us: local(): local_tiles = trailing.reshape(row_tiles, tile_size, col_tiles, tile_size)]
    dot_general x36 -> x0, matrix products: 156 us -> none  [the longest x2 126 us: full_update(): jnp.einsum('iab,jcb->iajc', panel_tiles, across, precision=lax.Precision....]
    unnamed x39 -> x43, local copies, waits for them, and re-layouts: 92.5 us -> 11.6 us
    select_n x6 -> x16, other arithmetic: 13.2 us -> 48.7 us  [the longest x9 12.3 us: local(): send = jnp.where(z == 0, head, arrived)]
  transfers between devices with their start and end apart: 6 -> 14, of which waited for: 5 -> 9; matrix products, arithmetic and copies ran while one was open for 6% -> 8% of each run, Pallas kernels for 0% -> 19%
where the time goes in v1:
time: 702 us; the launch traced here: 693 us
  waiting for transfers between devices  317 us (45%)
  Pallas kernels  240 us (34%)
  other arithmetic  70.8 us (10%)
  local copies, waits for them, and re-layouts  33.5 us (5%)
  starting transfers between devices  17.9 us (3%)
  between operations  14 us (2%)
    ppermute x10, waiting for transfers between devices, local(): arrived = lax.ppermute(send, 'row', [(x, x + 2) for x in range(n_row - 2)])  136 us
    pallas_call x4, Pallas kernels, factor_part(): pl.pallas_call(functools.partial(factor_kernel, stages), out_shape=jax.Sh...  109 us
    psum x1, waiting for transfers between devices, local(): seed = lax.psum(jnp.stack(seed), ('row', 'col'))  101 us
    pallas_call x2, Pallas kernels, solve(): pl.pallas_call(kernel, out_shape=[jax.ShapeDtypeStruct((m, *shape), dtype...  69.6 us
    pallas_call x1, Pallas kernels, update(): pl.pallas_call(functools.partial(update_kernel, n_row, n_col), out_shape=...  61.6 us
    ppermute x1, waiting for transfers between devices, local(): other = lax.ppermute(held, 'col', [(x, x ^ 1) for x in range(n_col)])  59.4 us
    ppermute x1, waiting for transfers between devices, local(): more = lax.ppermute(held, 'col', [(x, x + d) for x in range(d)])  20.5 us
    ppermute x10, starting transfers between devices, local(): arrived = lax.ppermute(send, 'row', [(x, x + 2) for x in range(n_row - 2)])  14.1 us
  transfers between devices with their start and end apart: 14, of which 9 were waited for; matrix products, arithmetic and copies ran while one was open for 8% of the time, Pallas kernels for 19%

profile of v1, /device:TPU:28, one launch (start us, length us, event | category | flops | bytes accessed | tf_op | source)
XLA Modules:
  0.0 693.1 jit_solution(8268684751042401689)
XLA Ops:
  6.5 9.4 %fusion.12 = (f32[1,1,512,1,1,512]{5,4,3,2,1,0:T(1,128)S(1)}, f32[1,1,512,1,1,512]{5,4,3,2,1,0:T(1,128)}, f32[1,1,512,1,1,512]{5,4,3,2,1,0:T(1,128)}, f32[1,1,51...) fusion(f32[4,1,512,8,1,512]{5,4,3,2,1,0:T(1,128)} %a_ref.1), kind=kLoop, calls=%fused_computation.52 | loop fusion | bytes 16777216 | tf_op jit(solution)/shard_map/slice | solution.py:227
  16.9 2.3 select_bitcast_fusion.2
  20.5 25.8 %collective-permute-done = f32[512,512]{1,0:T(8,128)} collective-permute-done((f32[512,512]{1,0:T(8,128)}, f32[512,512]{1,0:T(8,128)}, u32[]{:S(2)}, u32[]{:S(2)}) %collective-permute-start) | collective-permute-done | bytes 1048608 | tf_op jit(solution)/shard_map/ppermute | solution.py:245
  46.3 2.7 fusion.1
  50.3 3.9 pad_maximum_fusion
  54.2 34.9 %collective-permute-done.1 = f32[512,512]{1,0:T(8,128)} collective-permute-done((f32[512,512]{1,0:T(8,128)}, f32[512,512]{1,0:T(8,128)}, u32[]{:S(2)}, u32[]{:S(2)}) %collective-permute-start.1) | collective-permute-done | bytes 1048608 | tf_op jit(solution)/shard_map/ppermute | solution.py:245
  89.1 2.4 fusion
  91.6 1.5 collective-permute-start.2
  93.7 2.5 copy.68
  96.2 101.0 %all-reduce.2.cloned.1.call-done = f32[3,512,512]{2,1,0:T(8,128)} async-done(((f32[3,512,512]{2,1,0:T(8,128)}), f32[3,512,512]{2,1,0:T(8,128)}) %all-reduce.2.cloned.1.call-update) | async-done | bytes 3145744 | tf_op jit(solution)/shard_map/psum | solution.py:222
  197.2 3.0 slice_bitcast_fusion.1
  200.3 3.5 copy.9
  203.8 2.4 fusion.4
  207.5 2.8 slice_bitcast_fusion.2
  210.3 2.5 copy.10
  212.9 2.5 maximum_maximum_fusion.a_ref
  215.4 31.1 %factor.4.a_ref = f32[1024,1024]{1,0:T(8,128)S(1)} custom-call(s32[1]{0:T(128)} %constant.69.clone.1.at_ref, f32[1024,1024]{1,0:T(8,128)S(1)} %maximum_maximum_fusion.a_ref), custom_call_target="tpu_custom_call" | custom-call | flops 15000000512 | bytes 8388608 | tf_op jit(solution)/shard_map/factor/pallas_call | solution.py:82
  246.5 1.4 fusion.3
  248.0 1.9 collective-permute-start.6
  249.9 28.5 %factor.5.a_ref = f32[1024,1024]{1,0:T(8,128)S(1)} custom-call(s32[1]{0:T(128)} %constant.70.clone.1.at_ref, f32[1024,1024]{1,0:T(8,128)S(1)} %factor.4.a_ref), custom_call_target="tpu_custom_call" | custom-call | flops 15000000512 | bytes 8388608 | tf_op jit(solution)/shard_map/factor/pallas_call | solution.py:82
  280.1 26.0 %factor.6.a_ref = f32[1024,1024]{1,0:T(8,128)S(1)} custom-call(s32[1]{0:T(128)} %constant.71.clone.1.at_ref, f32[1024,1024]{1,0:T(8,128)S(1)} %factor.5.a_ref), custom_call_target="tpu_custom_call" | custom-call | flops 15000000512 | bytes 8388608 | tf_op jit(solution)/shard_map/factor/pallas_call | solution.py:82
  306.1 2.0 copy-done.2
  310.6 25.3 %collective-permute-done.8 = f32[512,512]{1,0:T(8,128)S(1)} collective-permute-done((f32[512,512]{1,0:T(8,128)S(1)}, f32[512,512]{1,0:T(8,128)S(1)}, u32[]{:S(2)}, u32[]{:S(2)}) %collective-permute-start.8) | collective-permute-done | bytes 1048608 | tf_op jit(solution)/shard_map/ppermute | solution.py:245
  340.8 2.7 bitcast_dynamic-update-slice_fusion.7
  343.5 18.6 %collective-permute-done.9 = f32[512,512]{1,0:T(8,128)} collective-permute-done((f32[512,512]{1,0:T(8,128)}, f32[512,512]{1,0:T(8,128)}, u32[]{:S(2)}, u32[]{:S(2)}) %collective-permute-start.9) | collective-permute-done | bytes 1048608 | tf_op jit(solution)/shard_map/ppermute | solution.py:245
  365.0 2.7 bitcast_dynamic-update-slice_fusion.6
  367.8 1.5 bitcast_dynamic-update-slice_fusion.5
  369.2 1.5 bitcast_dynamic-update-slice_fusion.4
  370.8 15.9 %collective-permute-done.10 = f32[512,512]{1,0:T(8,128)S(1)} collective-permute-done((f32[512,512]{1,0:T(8,128)S(1)}, f32[512,512]{1,0:T(8,128)S(1)}, u32[]{:S(2)}, u32[]{:S(2)}) %collective-permute-start.10) | collective-permute-done | bytes 1048608 | tf_op jit(solution)/shard_map/ppermute | solution.py:245
  388.3 1.5 bitcast_dynamic-update-slice_fusion.3
  389.7 2.7 bitcast_dynamic-update-slice_fusion.2
  392.4 1.5 bitcast_dynamic-update-slice_fusion.1
  393.9 15.1 %collective-permute-done.11 = f32[512,512]{1,0:T(8,128)S(1)} collective-permute-done((f32[512,512]{1,0:T(8,128)S(1)}, f32[512,512]{1,0:T(8,128)S(1)}, u32[]{:S(2)}, u32[]{:S(2)}) %collective-permute-start.11) | collective-permute-done | bytes 1048608 | tf_op jit(solution)/shard_map/ppermute | solution.py:245
  409.1 1.5 bitcast_dynamic-update-slice_fusion
  410.6 20.5 %collective-permute-done.3 = f32[4,512,512]{2,1,0:T(8,128)} collective-permute-done((f32[4,512,512]{2,1,0:T(8,128)}, f32[4,512,512]{2,1,0:T(8,128)}, u32[]{:S(2)}, u32[]{:S(2)}) %collective-permute-start.3) | collective-permute-done | bytes 4194336 | tf_op jit(solution)/shard_map/ppermute | solution.py:269
  431.0 5.3 broadcast_select_fusion.2
  436.4 2.4 collective-permute-start.4
  438.9 2.2 copy-done.3
  441.1 23.6 %factor.7 = f32[1024,1024]{1,0:T(8,128)S(1)} custom-call(s32[1]{0:T(128)} %constant.68.clone.1.at_ref, f32[1024,1024]{1,0:T(8,128)S(1)} %copy-done.3), custom_call_target="tpu_custom_call" | custom-call | flops 15000000512 | bytes 8388608 | tf_op jit(solution)/shard_map/factor/pallas_call | solution.py:82
  464.7 2.4 compare_select_fusion.w_ref
  467.1 59.4 %collective-permute-done.4 = f32[4,512,512]{2,1,0:T(8,128)} collective-permute-done((f32[4,512,512]{2,1,0:T(8,128)}, f32[4,512,512]{2,1,0:T(8,128)}, u32[]{:S(2)}, u32[]{:S(2)}) %collective-permute-start.4) | collective-permute-done | bytes 4194336 | tf_op jit(solution)/shard_map/ppermute | solution.py:272
  526.5 8.2 %broadcast_select_fusion.3 = (f32[4,512,512]{2,1,0:T(8,128)}, f32[4,512,512]{2,1,0:T(8,128)}) fusion(f32[4,512,512]{2,1,0:T(8,128)} %collective-permute-done.4, f32[4,512,512]{2,1,0:T(8,128)} %broadcast_select_fusion.2, pred[]{:T(512)S(6)} %eq.30), kind=kLoop, calls=%fused_computation.8 | loop fusion | flops 2097152 | bytes 16777216 | tf_op jit(solution)/shard_map/jit(_where)/select_n | solution.py:275
  534.7 25.0 %rows.1 = (f32[4,512,1024]{2,1,0:T(8,128)}, bf16[4,512,1024]{2,1,0:T(8,128)(2,1)S(1)}, bf16[4,512,1024]{2,1,0:T(8,128)(2,1)S(1)}) custom-call(f32[4,512,512]{2,1,0:T(8,128)} %get-tuple-element.44.x_ref, f32[4,512,512]{2,1,0:T(8,128)} %get-tuple-element.43.y_ref, f32[1024,1024]{1,0:T(8,128)} %compare_select_fusion.w_ref), custom_call_target="tpu_custom_call" | custom-call | flops 19327352832 | bytes 25165824 | tf_op jit(solution)/shard_map/rows/pallas_call | solution.py:137
  559.6 2.0 copy-done.1
  561.6 6.8 select_select_fusion.new_ref
  568.4 11.4 %broadcast_select_fusion = (f32[8,512,512]{2,1,0:T(8,128)}, f32[8,512,512]{2,1,0:T(8,128)}) fusion(f32[8,512,512]{2,1,0:T(8,128)} %collective-permute-done.12, f32[8,512,512]{2,1,0:T(8,128)} %bitcast_dynamic-update-slice_fusion, pred[]{:T(512)S(6)} %eq.36), kind=kLoop, calls=%fused_computation.3 | loop fusion | flops 4194304 | bytes 33554432 | tf_op jit(solution)/shard_map/jit(_where)/select_n | solution.py:265
  579.8 44.6 %cols.1 = (bf16[8,1024,512]{2,1,0:T(8,128)(2,1)}, bf16[8,1024,512]{2,1,0:T(8,128)(2,1)}) custom-call(f32[8,512,512]{2,1,0:T(8,128)} %get-tuple-element.42.x_ref, f32[8,512,512]{2,1,0:T(8,128)} %get-tuple-element.41.y_ref, f32[1024,1024]{1,0:T(8,128)S(1)} %copy-done), custom_call_target="tpu_custom_call" | custom-call | flops 38654705664 | bytes 50331648 | tf_op jit(solution)/shard_map/cols/pallas_call | solution.py:137
  624.5 61.6 %update.1 = f32[4,1,512,8,1,512]{5,4,3,2,1,0:T(1,128)} custom-call(s32[2]{0:T(128)S(1)} %pad_add_fusion.at_ref, f32[4,1,512,8,1,512]{5,4,3,2,1,0:T(1,128)} %a_ref.1, bf16[4,512,1024]{2,1,0:T(8,128)(2,1)S(1)} %get-tuple-element.27.ph_ref, bf16[4,512,1024]{2,1,0:T(8,128)(2,1)} %copy-done.1, bf16[8,1024,512]{2,1,0:T(8,128)(2,1)} %get-tuple-element.30.qh_ref, ...), custom_call_target="tpu_custom_call" | custom-call | tf_op jit(solution)/shard_map/update/pallas_call | solution.py:185
  (67 shorter events, 19.2 us)
Async XLA Ops:
  6.5 190.7 %all-reduce.2.cloned.1.call-start = ((), (), s32[]{:S(2)}) async-start(), calls=%async_computation | async-start | bytes 6291456 | tf_op jit(solution)/shard_map/psum | solution.py:222
  15.9 1.0 copy-start.20
  15.9 73.2 %copy-start.17 = (f32[1,1,512,1,1,512]{5,4,3,2,1,0:T(1,128)}, f32[1,1,512,1,1,512]{5,4,3,2,1,0:T(1,128)S(1)}, u32[]{:S(2)}) copy-start(f32[1,1,512,1,1,512]{5,4,3,2,1,0:T(1,128)S(1)} %get-tuple-element.39) | copy-start | bytes 3145732
  19.2 27.1 %collective-permute-start = (f32[512,512]{1,0:T(8,128)}, f32[512,512]{1,0:T(8,128)}, u32[]{:S(2)}, u32[]{:S(2)}) collective-permute-start(f32[512,512]{1,0:T(8,128)} %get-tuple-element.52), channel_id=1, source_target_pairs={{0,8},{4,12},{8,16},{12,20},{16,24},{20,28},{1,9},{5,13},{9,17},{1... | collective-permute-start | bytes 3145736 | tf_op jit(solution)/shard_map/ppermute | solution.py:245
  49.1 40.1 %collective-permute-start.1 = (f32[512,512]{1,0:T(8,128)}, f32[512,512]{1,0:T(8,128)}, u32[]{:S(2)}, u32[]{:S(2)}) collective-permute-start(f32[512,512]{1,0:T(8,128)} %fusion.1), channel_id=1, source_target_pairs={{0,8},{4,12},{8,16},{12,20},{16,24},{20,28},{1,9},{5,13},{9,17},{1... | collective-permute-start | bytes 3145736 | tf_op jit(solution)/shard_map/ppermute | solution.py:245
  91.6 2.2 slice-start
  91.6 105.7 %collective-permute-start.2 = (f32[512,512]{1,0:T(8,128)}, f32[512,512]{1,0:T(8,128)S(1)}, u32[]{:S(2)}, u32[]{:S(2)}) collective-permute-start(f32[512,512]{1,0:T(8,128)} %fusion), channel_id=1, source_target_pairs={{0,8},{4,12},{8,16},{12,20},{16,24},{20,28},{1,9},{5,13},{9,17},{1... | collective-permute-start | bytes 3145736 | tf_op jit(solution)/shard_map/ppermute | solution.py:245
  206.2 40.3 %collective-permute-start.5 = (f32[512,512]{1,0:T(8,128)}, f32[512,512]{1,0:T(8,128)}, u32[]{:S(2)}, u32[]{:S(2)}) collective-permute-start(f32[512,512]{1,0:T(8,128)} %fusion.4), channel_id=1, source_target_pairs={{0,8},{4,12},{8,16},{12,20},{16,24},{20,28},{1,9},{5,13},{9,17},{1... | collective-permute-start | bytes 3145736 | tf_op jit(solution)/shard_map/ppermute | solution.py:245
  215.4 31.1 %copy-start.14 = (f32[1,1,512,1,1,512]{5,4,3,2,1,0:T(1,128)S(1)}, f32[1,1,512,1,1,512]{5,4,3,2,1,0:T(1,128)}, u32[]{:S(2)}) copy-start(f32[1,1,512,1,1,512]{5,4,3,2,1,0:T(1,128)} %get-tuple-element.35) | copy-start | bytes 3145732
  248.0 30.5 %copy-start.12 = (f32[1,1,512,1,1,512]{5,4,3,2,1,0:T(1,128)S(1)}, f32[1,1,512,1,1,512]{5,4,3,2,1,0:T(1,128)}, u32[]{:S(2)}) copy-start(f32[1,1,512,1,1,512]{5,4,3,2,1,0:T(1,128)} %get-tuple-element.36) | copy-start | bytes 3145732
  248.0 30.4 %collective-permute-start.6 = (f32[512,512]{1,0:T(8,128)S(1)}, f32[512,512]{1,0:T(8,128)S(1)}, u32[]{:S(2)}, u32[]{:S(2)}) collective-permute-start(f32[512,512]{1,0:T(8,128)S(1)} %fusion.3), channel_id=1, source_target_pairs={{0,8},{4,12},{8,16},{12,20},{16,24},{20,28},{1,9},{5,13},{9,17},{1... | collective-permute-start | bytes 3145736 | tf_op jit(solution)/shard_map/ppermute | solution.py:245
  278.4 27.7 %copy-start.4 = (f32[512,512]{1,0:T(8,128)}, f32[512,512]{1,0:T(8,128)S(1)}, u32[]{:S(2)}) copy-start(f32[512,512]{1,0:T(8,128)S(1)} %collective-permute-done.6) | copy-start | bytes 3145732
  278.7 30.4 %copy-start.10 = (f32[1,1,512,1,1,512]{5,4,3,2,1,0:T(1,128)S(1)}, f32[1,1,512,1,1,512]{5,4,3,2,1,0:T(1,128)}, u32[]{:S(2)}) copy-start(f32[1,1,512,1,1,512]{5,4,3,2,1,0:T(1,128)} %get-tuple-element.40) | copy-start | bytes 3145732
  278.7 29.4 %collective-permute-start.7 = (f32[512,512]{1,0:T(8,128)S(1)}, f32[512,512]{1,0:T(8,128)S(1)}, u32[]{:S(2)}, u32[]{:S(2)}) collective-permute-start(f32[512,512]{1,0:T(8,128)S(1)} %fusion.2), channel_id=1, source_target_pairs={{0,8},{4,12},{8,16},{12,20},{16,24},{20,28},{1,9},{5,13},{9,17},{1... | collective-permute-start | bytes 3145736 | tf_op jit(solution)/shard_map/ppermute | solution.py:245
  306.1 2.0 copy-start.2
  308.1 1.0 copy-start.6
  309.3 26.6 %collective-permute-start.8 = (f32[512,512]{1,0:T(8,128)S(1)}, f32[512,512]{1,0:T(8,128)S(1)}, u32[]{:S(2)}, u32[]{:S(2)}) collective-permute-start(f32[512,512]{1,0:T(8,128)S(1)} %fusion.5), channel_id=1, source_target_pairs={{0,8},{4,12},{8,16},{12,20},{16,24},{20,28},{1,9},{5,13},{9,17},{1... | collective-permute-start | bytes 3145736 | tf_op jit(solution)/shard_map/ppermute | solution.py:245
  335.9 1.0 copy-start.8
  338.1 24.1 %collective-permute-start.9 = (f32[512,512]{1,0:T(8,128)}, f32[512,512]{1,0:T(8,128)}, u32[]{:S(2)}, u32[]{:S(2)}) collective-permute-start(f32[512,512]{1,0:T(8,128)} %fusion.8), channel_id=1, source_target_pairs={{0,8},{4,12},{8,16},{12,20},{16,24},{20,28},{1,9},{5,13},{9,17},{1... | collective-permute-start | bytes 3145736 | tf_op jit(solution)/shard_map/ppermute | solution.py:245
  339.3 25.7 %copy-start.19 = (f32[1,1,512,1,1,512]{5,4,3,2,1,0:T(1,128)S(1)}, f32[1,1,512,1,1,512]{5,4,3,2,1,0:T(1,128)}, u32[]{:S(2)}) copy-start(f32[1,1,512,1,1,512]{5,4,3,2,1,0:T(1,128)} %get-tuple-element.38) | copy-start | bytes 3145732
  339.4 91.7 %collective-permute-start.3 = (f32[4,512,512]{2,1,0:T(8,128)}, f32[4,512,512]{2,1,0:T(8,128)}, u32[]{:S(2)}, u32[]{:S(2)}) collective-permute-start(f32[4,512,512]{2,1,0:T(8,128)} %bitcast.86), channel_id=1, source_target_pairs={{0,2},{1,3},{4,6},{5,7},{8,10},{9,11},{12,14},{13,15},{16,18},{17,... | collective-permute-start | bytes 12582920 | tf_op jit(solution)/shard_map/ppermute | solution.py:269
  343.5 24.3 %copy-start.5 = (f32[512,512]{1,0:T(8,128)S(1)}, f32[512,512]{1,0:T(8,128)}, u32[]{:S(2)}) copy-start(f32[512,512]{1,0:T(8,128)} %copy-done.4) | copy-start | bytes 3145732
  343.5 24.3 %copy-start.18 = (f32[1,1,512,1,1,512]{5,4,3,2,1,0:T(1,128)S(1)}, f32[1,1,512,1,1,512]{5,4,3,2,1,0:T(1,128)}, u32[]{:S(2)}) copy-start(f32[1,1,512,1,1,512]{5,4,3,2,1,0:T(1,128)} %copy-done.17) | copy-start | bytes 3145732
  363.6 5.6 copy-start.7
  363.6 5.6 copy-start.16
  363.6 23.0 %collective-permute-start.10 = (f32[512,512]{1,0:T(8,128)S(1)}, f32[512,512]{1,0:T(8,128)S(1)}, u32[]{:S(2)}, u32[]{:S(2)}) collective-permute-start(f32[512,512]{1,0:T(8,128)S(1)} %fusion.7), channel_id=1, source_target_pairs={{0,8},{4,12},{8,16},{12,20},{16,24},{20,28},{1,9},{5,13},{9,17},{1... | collective-permute-start | bytes 3145736 | tf_op jit(solution)/shard_map/ppermute | solution.py:245
  369.2 19.0 %copy-start.9 = (f32[512,512]{1,0:T(8,128)S(1)}, f32[512,512]{1,0:T(8,128)}, u32[]{:S(2)}) copy-start(f32[512,512]{1,0:T(8,128)} %copy-done.8) | copy-start | bytes 3145732
  369.2 19.0 %copy-start.15 = (f32[1,1,512,1,1,512]{5,4,3,2,1,0:T(1,128)S(1)}, f32[1,1,512,1,1,512]{5,4,3,2,1,0:T(1,128)}, u32[]{:S(2)}) copy-start(f32[1,1,512,1,1,512]{5,4,3,2,1,0:T(1,128)} %get-tuple-element.35) | copy-start | bytes 3145732
  370.8 19.0 %copy-start.13 = (f32[1,1,512,1,1,512]{5,4,3,2,1,0:T(1,128)S(1)}, f32[1,1,512,1,1,512]{5,4,3,2,1,0:T(1,128)}, u32[]{:S(2)}) copy-start(f32[1,1,512,1,1,512]{5,4,3,2,1,0:T(1,128)} %get-tuple-element.36) | copy-start | bytes 3145732
  386.8 5.6 copy-start.11
  386.8 22.2 %collective-permute-start.11 = (f32[512,512]{1,0:T(8,128)S(1)}, f32[512,512]{1,0:T(8,128)S(1)}, u32[]{:S(2)}, u32[]{:S(2)}) collective-permute-start(f32[512,512]{1,0:T(8,128)S(1)} %fusion.6), channel_id=1, source_target_pairs={{0,8},{4,12},{8,16},{12,20},{16,24},{20,28},{1,9},{5,13},{9,17},{1... | collective-permute-start | bytes 3145736 | tf_op jit(solution)/shard_map/ppermute | solution.py:245
  410.5 157.8 %collective-permute-start.12 = (f32[8,512,512]{2,1,0:T(8,128)}, f32[8,512,512]{2,1,0:T(8,128)}, u32[]{:S(2)}, u32[]{:S(2)}) collective-permute-start(f32[8,512,512]{2,1,0:T(8,128)} %bitcast_dynamic-update-slice_fusion), channel_id=1, source_target_pairs={{0,4},{4,0},{8,12},{12,8},{16,20},{20,16},{24,28},{28,24},{1,5},{5... | collective-permute-start | bytes 25165832 | tf_op jit(solution)/shard_map/ppermute | solution.py:262
  436.4 90.1 %collective-permute-start.4 = (f32[4,512,512]{2,1,0:T(8,128)}, f32[4,512,512]{2,1,0:T(8,128)}, u32[]{:S(2)}, u32[]{:S(2)}) collective-permute-start(f32[4,512,512]{2,1,0:T(8,128)} %broadcast_select_fusion.2), channel_id=1, source_target_pairs={{0,1},{1,0},{2,3},{3,2},{4,5},{5,4},{6,7},{7,6},{8,9},{9,8},{10,11... | collective-permute-start | bytes 12582920 | tf_op jit(solution)/shard_map/ppermute | solution.py:272
  438.9 2.2 copy-start.3
  559.6 2.0 copy-start.1
  568.4 11.4 %copy-start = (f32[1024,1024]{1,0:T(8,128)S(1)}, f32[1024,1024]{1,0:T(8,128)}, u32[]{:S(2)}) copy-start(f32[1024,1024]{1,0:T(8,128)} %compare_select_fusion.w_ref) | copy-start | bytes 12582916
Sparse Core Ops, SparseCore 0:
  54.3 142.8 all-reduce.1
